TPU v7x, 128 devices: a whole 4x4x4 slice. The times are simulated.
128 devices in a mesh: pts: 16 (over x, z), nbr: 8 (over y, core).
Axes of the slice: x: 4, y: 4, z: 4, core: 2. Of those that a mesh axis runs over, the one named last changes fastest.
Arguments:
- points: bfloat16 [16, 8, 4096, 128], P('pts', 'nbr'), may hold values from -6 to 6
- dest_owner: int32 [16, 8, 4096, 1], P('pts', 'nbr'), may hold values from 0 to 127; in each aligned block of 4096 rows (0 to 4095, 4096 to 8191, ..., all dimensions but the last counted through in order) at most 64 rows name the same one
- dest_cell: int32 [16, 8, 4096], P('pts', 'nbr'), may hold values from 0 to 8191
- level_input: bfloat16 [128, 512, 16, 128], P('nbr', 'pts'), may hold values from -6 to 6
- w_res: bfloat16 [27, 128, 128], replicated, may hold values from -0.109375 to 0.109375
- w_down: bfloat16 [27, 128, 256], replicated, may hold values from -0.109375 to 0.109375
Outputs:
- lowered: bfloat16 [64, 256, 8, 256], P('nbr', 'pts')
Inputs may be any that keep to these rules, and one draw needn't show every extreme that they name: `dest_owner`: at most 64 points of one device go to one owner, and some device sends exactly 64 points to some owner.
All inputs are finite; a program needn't handle non-finite values.
Results may differ from a plain program's by a relative error of at most 0.0048.
Values may be sent and summed in bfloat16 or wider, within the bound.
A program may use at most 64 MiB of HBM per device.

v0:
```python
import functools

import jax
import jax.numpy as jnp
from jax import lax
from jax.experimental import pallas as pl
from jax.experimental.pallas import tpu as pltpu
from jax.sharding import PartitionSpec as P

MESH = pl.DeviceIdType.MESH
F32, BF16, I32 = jnp.float32, jnp.bfloat16, jnp.int32
DEV, CAP, ROWS, C = 128, 64, 4096, 128
NX, NY, NZ = 16, 32, 16
CELLS = NX * NY * NZ
CHAINS = 4
VMEM = pl.BlockSpec(memory_space=pltpu.VMEM)
SMEM = pl.BlockSpec(memory_space=pltpu.SMEM)
ANY = pl.BlockSpec(memory_space=pl.ANY)


def slots_kernel(own_ref, cell_ref, idx_ref, cells_ref, hit_ref, val_ref):
    block = 256
    hit_ref[...] = (lax.broadcasted_iota(I32, (DEV, ROWS), 0) == own_ref[...]).astype(F32).astype(BF16)
    before = (
        lax.broadcasted_iota(I32, (block, block), 0) < lax.broadcasted_iota(I32, (block, block), 1)
    ).astype(F32).astype(BF16)
    carry = jnp.zeros((DEV, 1), F32)
    for b in range(ROWS // block):
        span = slice(b * block, (b + 1) * block)
        hit = hit_ref[:, span]
        hit32 = hit.astype(F32)
        ranks = jnp.dot(hit, before, preferred_element_type=F32) + carry
        rank = jnp.sum(ranks * hit32, axis=0, keepdims=True).astype(I32)
        carry = carry + jnp.sum(hit32, axis=1, keepdims=True)
        place = lax.broadcasted_iota(I32, (CAP, block), 0) == rank
        row = lax.broadcasted_iota(I32, (1, block), 1) + b * block
        cell = cell_ref[:, span]
        for part, value in enumerate((row % 64, row // 64, cell % 64, cell // 64 + 1)):
            chosen = jnp.where(place, value.astype(F32), 0.0)
            val_ref[part * CAP : (part + 1) * CAP, span] = chosen.astype(BF16)
    found = lax.dot_general(
        hit_ref[...], val_ref[...], (((1,), (1,)), ((), ())), preferred_element_type=F32
    ).astype(I32)
    idx_ref[...] = found[:, CAP : 2 * CAP] * 64 + found[:, :CAP]
    high = found[:, 3 * CAP :]
    cell = (high - 1) * 64 + found[:, 2 * CAP : 3 * CAP]
    cells_ref[:, :CAP] = jnp.where(high > 0, cell, CELLS)
    cells_ref[:, CAP:] = jnp.full((DEV, CAP), CELLS, I32)


def find_slots(own, cell):
    return pl.pallas_call(
        slots_kernel,
        out_shape=(
            jax.ShapeDtypeStruct((DEV, CAP), I32),
            jax.ShapeDtypeStruct((DEV, 2 * CAP), I32),
        ),
        in_specs=[VMEM, VMEM],
        out_specs=(VMEM, VMEM),
        scratch_shapes=[pltpu.VMEM((DEV, ROWS), BF16), pltpu.VMEM((4 * CAP, ROWS), BF16)],
        compiler_params=pltpu.CompilerParams(vmem_limit_bytes=32 << 20),
    )(own, cell)


def partner(k, p, n):
    t = (k * 37) % DEV
    dx, dz, dy, dc = t % 4, (t // 4) % 4, (t // 16) % 4, t // 64
    return (p // 4 + dx) % 4 * 4 + (p % 4 + dz) % 4, (n // 2 + dy) % 4 * 2 + (n % 2 + dc) % 2


def exchange_kernel(
    idx_ref, cells_ref, pts_ref, level_ref, w_ref,
    got_ref, got_cells_ref, base_ref,
    rows32, packed, ext, s0, s1, s2, wide, base,
    row_send, row_recv, cell_send, cell_recv, own_sem, own_cell_sem, in_sem, halo_send, halo_recv, out_sem,
):
    p, n = lax.axis_index("pts"), lax.axis_index("nbr")
    n_p, n_n = lax.axis_size("pts"), lax.axis_size("nbr")
    me = p * n_n + n
    barrier = pltpu.get_barrier_semaphore()

    def greet(k, carry):
        tp, tn = partner(k, p, n)
        pl.semaphore_signal(barrier, inc=1, device_id=(tp, tn), device_id_type=MESH)
        return carry

    lax.fori_loop(1, DEV, greet, 0)
    inner = pltpu.make_async_copy(level_ref, ext.at[pl.ds(1, NX), pl.ds(1, NY)], in_sem)
    inner.start()
    rows32[...] = pts_ref[...].astype(F32)

    def gather(owner):
        for g in range(CAP // 16):
            rows = [rows32[pl.ds(idx_ref[owner, g * 16 + r], 1), :] for r in range(16)]
            packed[owner, g * 16 : (g + 1) * 16, :] = jnp.concatenate(rows, axis=0).astype(BF16)

    gather(me)
    own = pltpu.make_async_copy(packed.at[me], got_ref.at[me], own_sem)
    own.start()
    own_cells = pltpu.make_async_copy(cells_ref.at[me], got_cells_ref.at[me], own_cell_sem)
    own_cells.start()
    pl.semaphore_wait(barrier, DEV - 1)

    sides = []
    for dn in (-1, 0, 1):
        for dp in (-1, 0, 1):
            if dn == 0 and dp == 0:
                continue
            sx = pl.ds(0, NX) if dn == 0 else pl.ds(NX - 1 if dn > 0 else 0, 1)
            sy = pl.ds(0, NY) if dp == 0 else pl.ds(NY - 1 if dp > 0 else 0, 1)
            tx = pl.ds(1, NX) if dn == 0 else pl.ds(0 if dn > 0 else NX + 1, 1)
            ty = pl.ds(1, NY) if dp == 0 else pl.ds(0 if dp > 0 else NY + 1, 1)
            at = len(sides)
            to_n, to_p, from_n, from_p = n + dn, p + dp, n - dn, p - dp
            there = (to_n >= 0) & (to_n < n_n) & (to_p >= 0) & (to_p < n_p)
            here = (from_n >= 0) & (from_n < n_n) & (from_p >= 0) & (from_p < n_p)
            copy = pltpu.make_async_remote_copy(
                level_ref.at[sx, sy], ext.at[tx, ty], halo_send.at[at], halo_recv.at[at],
                device_id=((p + dp + n_p) % n_p, (n + dn + n_n) % n_n), device_id_type=MESH,
            )
            sides.append((there, here, copy, tx, ty))

            @pl.when(there)
            def _():
                copy.start()

    def send(k, carry):
        tp, tn = partner(k, p, n)
        owner = tp * n_n + tn
        gather(owner)
        pltpu.make_async_remote_copy(
            packed.at[owner], got_ref.at[me], row_send, row_recv, device_id=(tp, tn), device_id_type=MESH
        ).start()
        pltpu.make_async_remote_copy(
            cells_ref.at[owner], got_cells_ref.at[me], cell_send, cell_recv,
            device_id=(tp, tn), device_id_type=MESH,
        ).start()
        return carry

    lax.fori_loop(1, DEV, send, 0)

    for a in range(3):
        for q in range(2):
            for c in range(3):
                for pin in range(2):
                    for pout in range(2):
                        b = 2 * q + pin - pout
                        at = (a * 2 + q) * 3 + c
                        tap = w_ref[9 * a + 3 * b + c] if 0 <= b <= 2 else jnp.zeros((C, C), BF16)
                        wide[at * 256 + pin * C : at * 256 + (pin + 1) * C, pout * C : (pout + 1) * C] = tap

    inner.wait()
    for there, here, copy, tx, ty in sides:
        shape = (tx.size, ty.size, NZ, C)

        @pl.when(here)
        def _():
            copy.wait_recv()

        @pl.when(jnp.logical_not(here))
        def _():
            ext[tx, ty] = jnp.zeros(shape, BF16)

    def shift(x, carry):
        for q in range(NY // 2 + 1):
            for part in range(2):
                line = ext[x, 2 * q + part]
                line32 = line.astype(F32)
                edge = jnp.zeros((1, C), F32)
                lanes = slice(part * C, (part + 1) * C)
                s1[x, q, :, lanes] = line
                s0[x, q, :, lanes] = jnp.concatenate([edge, line32[: NZ - 1]], axis=0).astype(BF16)
                s2[x, q, :, lanes] = jnp.concatenate([line32[1:], edge], axis=0).astype(BF16)
        return carry

    lax.fori_loop(0, NX + 2, shift, 0)

    half = NY // 2

    def conv(i, carry):
        lhs = jnp.concatenate(
            [
                s[i + a, q : q + half].reshape(half * NZ, 2 * C)
                for a in range(3)
                for q in range(2)
                for s in (s0, s1, s2)
            ],
            axis=1,
        )
        both = jnp.maximum(jnp.dot(lhs, wide[...], preferred_element_type=F32), 0.0)
        low = s1[i + 1, :half, :, C:].astype(F32)
        high = s1[i + 1, 1:, :, :C].astype(F32)
        base[i, :, 0] = both[:, :C].reshape(half, NZ, C) + low
        base[i, :, 1] = both[:, C:].reshape(half, NZ, C) + high
        pltpu.make_async_copy(base.at[i], base_ref.at[i], out_sem).start()
        return carry

    lax.fori_loop(0, NX, conv, 0)

    pltpu.make_async_copy(base, base_ref, out_sem).wait()
    own.wait()
    own_cells.wait()
    for there, here, copy, tx, ty in sides:

        @pl.when(there)
        def _():
            copy.wait_send()

    most = pl.ds(0, DEV - 1)
    pltpu.make_async_copy(packed.at[most], got_ref.at[most], row_send).wait()
    pltpu.make_async_copy(cells_ref.at[most], got_cells_ref.at[most], cell_send).wait()
    pltpu.make_async_copy(packed.at[most], got_ref.at[most], row_recv).wait()
    pltpu.make_async_copy(cells_ref.at[most], got_cells_ref.at[most], cell_recv).wait()


def exchange(idx, cells, pts, level, w_res):
    dma = pltpu.SemaphoreType.DMA
    padded = (NX + 2, NY // 2 + 1, NZ, 2 * C)
    return pl.pallas_call(
        exchange_kernel,
        out_shape=(
            jax.ShapeDtypeStruct((DEV, CAP, C), BF16),
            jax.ShapeDtypeStruct((DEV, 1, 2 * CAP), I32),
            jax.ShapeDtypeStruct((NX, NY // 2, 2, NZ, C), F32),
        ),
        in_specs=[SMEM, VMEM, VMEM, ANY, VMEM],
        out_specs=(ANY, ANY, ANY),
        scratch_shapes=[
            pltpu.VMEM((ROWS, C), F32),
            pltpu.VMEM((DEV, CAP, C), BF16),
            pltpu.VMEM((NX + 2, NY + 2, NZ, C), BF16),
            pltpu.VMEM(padded, BF16),
            pltpu.VMEM(padded, BF16),
            pltpu.VMEM(padded, BF16),
            pltpu.VMEM((18 * 256, 256), BF16),
            pltpu.VMEM((NX, NY // 2, 2, NZ, C), F32),
            dma, dma, dma, dma, dma, dma, dma, dma((8,)), dma((8,)), dma,
        ],
        compiler_params=pltpu.CompilerParams(
            collective_id=0, has_side_effects=True, vmem_limit_bytes=52 << 20
        ),
    )(idx, cells, pts, level, w_res)


def scatter_kernel(cells_ref, got_ref, base_ref, even_ref, odd_ref, last_ref, rows32, sem, *sums):
    first = pltpu.make_async_copy(base_ref, sums[0].at[pl.ds(0, CELLS)], sem)
    first.start()

    def clear(t, carry):
        span = pl.ds(pl.multiple_of(t * 32, 32), 32)
        for total in sums[1:]:
            total[span, :] = jnp.zeros((32, C), F32)
        rows32[span, :] = got_ref[span, :].astype(F32)
        return carry

    lax.fori_loop(0, CELLS // 32, clear, 0)
    first.wait()
    share = DEV // CHAINS

    def add(s, carry):
        for g in range(CAP // 16):
            for r in range(g * 16, g * 16 + 16):
                at = [cells_ref[k * share + s, r] for k in range(CHAINS)]
                new = [
                    sums[k][pl.ds(at[k], 1), :] + rows32[pl.ds((k * share + s) * CAP + r, 1), :]
                    for k in range(CHAINS)
                ]
                for k in range(CHAINS):
                    sums[k][pl.ds(at[k], 1), :] = new[k]
        return carry

    lax.fori_loop(0, share, add, 0)

    def deal(x, carry):
        top = lax.broadcasted_iota(I32, (NZ // 2, C), 0) == 0

        def total(y, start):
            at = pl.ds((x * NY + y) * NZ + start, NZ // 2, stride=2)
            value = sums[0][at, :]
            for more in sums[1:]:
                value = value + more[at, :]
            return value

        for parity, out_ref in ((0, even_ref), (1, odd_ref)):
            for j in range(0, NY // 2, 2):
                parts = []
                for y in (2 * j + parity, 2 * j + 2 + parity):
                    even, odd = total(y, 0), total(y, 1)
                    below = jnp.where(top, 0.0, pltpu.roll(odd, 1, 0))
                    parts.append((below, even, odd))
                for c in range(3):
                    pair = jnp.concatenate([parts[0][c], parts[1][c]], axis=0).astype(BF16)
                    out_ref[x, j * 8 : j * 8 + 16, c * C : (c + 1) * C] = pair
        return carry

    lax.fori_loop(0, NX, deal, 0)
    for x in range(0, NX, 2):
        parts = [odd_ref[x + h, 112:128, :].astype(F32)[8:] for h in range(2)]
        last_ref[x * 8 : x * 8 + 16, :] = jnp.concatenate(parts, axis=0).astype(BF16)


def scatter(cells, got, base):
    return pl.pallas_call(
        scatter_kernel,
        out_shape=(
            jax.ShapeDtypeStruct((NX, 128, 3 * C), BF16),
            jax.ShapeDtypeStruct((NX, 128, 3 * C), BF16),
            jax.ShapeDtypeStruct((128, 3 * C), BF16),
        ),
        in_specs=[SMEM, VMEM, ANY],
        out_specs=(VMEM, VMEM, VMEM),
        scratch_shapes=[pltpu.VMEM((CELLS, C), F32), pltpu.SemaphoreType.DMA]
        + [pltpu.VMEM((CELLS + 8, C), F32)] * CHAINS,
        compiler_params=pltpu.CompilerParams(vmem_limit_bytes=56 << 20),
    )(cells, got, base)


def lower_kernel(
    even_ref, odd_ref, last_ref, w_ref, out_ref,
    t0, t1, t2, side, corner, send_sem, recv_sem, in_sem,
):
    p, n = lax.axis_index("pts"), lax.axis_index("nbr")
    n_p, n_n = lax.axis_size("pts"), lax.axis_size("nbr")
    barrier = pltpu.get_barrier_semaphore()
    near = ((0, 1), (1, 0), (1, 1))
    up = [((p + dp) % n_p, (n + dn) % n_n) for dp, dn in near]
    down = [((p - dp + n_p) % n_p, (n - dn + n_n) % n_n) for dp, dn in near]
    for device in down:
        pl.semaphore_signal(barrier, inc=1, device_id=device, device_id_type=MESH)
    pl.semaphore_wait(barrier, 3)

    sent = [
        (0, even_ref.at[NX - 1], t1.at[0]),
        (0, odd_ref.at[NX - 1], t2.at[0]),
        (1, last_ref, side),
        (2, last_ref.at[pl.ds(112, 16)], corner),
    ]
    copies = []
    for at, (way, source, target) in enumerate(sent):
        dp, dn = near[way]
        there = (p + dp < n_p) & (n + dn < n_n)
        here = (p - dp >= 0) & (n - dn >= 0)
        copy = pltpu.make_async_remote_copy(
            source, target, send_sem.at[at], recv_sem.at[at], device_id=up[way], device_id_type=MESH
        )
        copies.append((there, here, copy, target))

        @pl.when(there)
        def _():
            copy.start()

    inner = [
        pltpu.make_async_copy(even_ref, t1.at[pl.ds(1, NX)], in_sem.at[0]),
        pltpu.make_async_copy(odd_ref, t2.at[pl.ds(1, NX)], in_sem.at[1]),
    ]
    for copy in inner:
        copy.start()
    for copy in inner:
        copy.wait()
    for there, here, copy, target in copies:

        @pl.when(here)
        def _():
            copy.wait_recv()

        @pl.when(jnp.logical_not(here))
        def _():
            target[...] = jnp.zeros(target.shape, BF16)

    def behind(x, edge):
        line = t2[x].astype(F32)
        t0[x] = jnp.concatenate([edge, line[:120]], axis=0).astype(BF16)

    behind(0, corner[...].astype(F32)[8:])
    for x in range(0, NX, 2):
        edges = side[x * 8 : x * 8 + 16, :].astype(F32)
        behind(x + 1, edges[:8])
        behind(x + 2, edges[8:])

    def conv(i, carry):
        lhs = jnp.concatenate(
            [
                jnp.concatenate([t[4 * i + a], t[4 * i + 2 + a]], axis=0)
                for a in range(3)
                for t in (t0, t1, t2)
            ],
            axis=1,
        )
        low = jnp.dot(lhs, w_ref[...], preferred_element_type=F32).astype(BF16)
        out_ref[2 * i] = low[:128]
        out_ref[2 * i + 1] = low[128:]
        return carry

    lax.fori_loop(0, NX // 4, conv, 0)
    for there, here, copy, target in copies:

        @pl.when(there)
        def _():
            copy.wait_send()


def lower(even, odd, last, w_down):
    dma = pltpu.SemaphoreType.DMA
    return pl.pallas_call(
        lower_kernel,
        out_shape=jax.ShapeDtypeStruct((NX // 2, 128, 2 * C), BF16),
        in_specs=[ANY, ANY, ANY, VMEM],
        out_specs=VMEM,
        scratch_shapes=[pltpu.VMEM((NX + 1, 128, 3 * C), BF16)] * 3
        + [pltpu.VMEM((128, 3 * C), BF16), pltpu.VMEM((16, 3 * C), BF16), dma((4,)), dma((4,)), dma((2,))],
        compiler_params=pltpu.CompilerParams(
            collective_id=1, has_side_effects=True, vmem_limit_bytes=48 << 20
        ),
    )(even, odd, last, w_down)


def body(points, dest_owner, dest_cell, level_input, w_res, w_down):
    idx, cells = find_slots(dest_owner.reshape(1, ROWS), dest_cell.reshape(1, ROWS))
    got, got_cells, base = exchange(
        idx, cells.reshape(DEV, 1, 2 * CAP), points.reshape(ROWS, C), level_input, w_res
    )
    even, odd, last = scatter(
        got_cells.reshape(DEV, 2 * CAP), got.reshape(DEV * CAP, C), base.reshape(CELLS, C)
    )
    lowered = lower(even, odd, last, w_down.reshape(27 * C, 2 * C))
    return lowered.reshape(NX // 2, NY // 2, NZ // 2, 2 * C)


def solution(mesh):
    return jax.shard_map(
        body,
        mesh=mesh,
        in_specs=(
            P("pts", "nbr", None, None),
            P("pts", "nbr", None, None),
            P("pts", "nbr", None),
            P("nbr", "pts", None, None),
            P(),
            P(),
        ),
        out_specs=P("nbr", "pts", None, None),
        check_vma=False,
    )
```

profile of v0, /device:TPU:11, one launch (start us, length us, event | category | flops | bytes accessed | tf_op | source)
XLA Modules:
  0.0 89.0 jit_solution(1433931848334452270)
XLA Ops:
  0.0 0.0 copy-start.6
  0.0 0.7 copy-done.6
  0.7 0.0 copy-start.7
  0.7 0.7 copy-done.7
  1.4 1.5 %shard_map.64 = (s32[128,64]{1,0:T(8,128)S(1)}, s32[128,128]{1,0:T(8,128)S(1)}) custom-call(s32[1,4096]{1,0:T(1,128)S(1)} %bitcast.13, s32[1,4096]{1,0:T(1,128)S(1)} %bitcast.14), custom_call_target="tpu_custom_call" | custom-call | tf_op jit(solution)/shard_map/pallas_call | solution.py:52
  3.0 0.0 copy-start.3
  3.0 1.2 %copy-done.3 = bf16[27,128,128]{2,1,0:T(8,128)(2,1)S(1)} copy-done((bf16[27,128,128]{2,1,0:T(8,128)(2,1)S(1)}, bf16[27,128,128]{2,1,0:T(8,128)(2,1)}, u32[]{:S(2)}) %copy-start.3) | copy-done | bytes 884760
  4.2 49.6 %shard_map.65 = (bf16[128,64,128]{2,1,0:T(8,128)(2,1)}, s32[128,1,128]{2,1,0:T(1,128)S(1)}, f32[16,16,2,16,128]{4,3,2,1,0:T(8,128)}) custom-call(s32[128,64]{1,0:T(8,128)S(1)} %get-tuple-element.13.idx_ref, s32[128,1,128]{2,1,0:T(1,128)S(1)} %bitcast.12, bf16[4096,128]{1,0:T(8,128)(2,1)} %bitcast.17, bf16[16,32,16,128]{3,2,1,0:T(8,128)(2,1)} %level_ref.1, ...), custom_call_target="tpu_custom_call" | custom-call | tf_op jit(solution)/shard_map/pallas_call | solution.py:219
  53.8 0.0 copy-start.5
  53.8 0.6 copy-done.5
  54.4 0.0 copy-start
  54.4 20.2 %shard_map.66 = (bf16[16,128,384]{2,1,0:T(8,128)(2,1)}, bf16[16,128,384]{2,1,0:T(8,128)(2,1)}, bf16[128,384]{1,0:T(8,128)(2,1)}) custom-call(s32[128,128]{1,0:T(8,128)} %bitcast.11, bf16[8192,128]{1,0:T(8,128)(2,1)} %bitcast.16, f32[8192,128]{1,0:T(8,128)} %bitcast.15), custom_call_target="tpu_custom_call" | custom-call | tf_op jit(solution)/shard_map/pallas_call | solution.py:303
  74.6 0.0 copy-done
  74.7 0.0 copy-start.1
  74.7 1.4 %copy-done.1 = bf16[16,128,384]{2,1,0:T(8,128)(2,1)S(1)} copy-done((bf16[16,128,384]{2,1,0:T(8,128)(2,1)S(1)}, bf16[16,128,384]{2,1,0:T(8,128)(2,1)}, u32[]{:S(2)}) %copy-start.1) | copy-done | bytes 1572888
  76.1 0.0 copy-start.2
  76.1 1.4 %copy-done.2 = bf16[16,128,384]{2,1,0:T(8,128)(2,1)S(1)} copy-done((bf16[16,128,384]{2,1,0:T(8,128)(2,1)S(1)}, bf16[16,128,384]{2,1,0:T(8,128)(2,1)}, u32[]{:S(2)}) %copy-start.2) | copy-done | bytes 1572888
  77.5 0.0 copy-start.4
  77.5 0.9 %copy-done.4 = bf16[128,384]{1,0:T(8,128)(2,1)S(1)} copy-done((bf16[128,384]{1,0:T(8,128)(2,1)S(1)}, bf16[128,384]{1,0:T(8,128)(2,1)}, u32[]{:S(2)}) %copy-start.4) | copy-done | bytes 98328
  78.4 9.9 %shard_map.67 = bf16[8,128,256]{2,1,0:T(8,128)(2,1)S(1)} custom-call(bf16[16,128,384]{2,1,0:T(8,128)(2,1)S(1)} %copy-done.1, bf16[16,128,384]{2,1,0:T(8,128)(2,1)S(1)} %copy-done.2, bf16[128,384]{1,0:T(8,128)(2,1)S(1)} %copy-done.4, bf16[3456,256]{1,0:T(8,128)(2,1)S(1)} %bitcast.10), custom_call_target="tpu_custom_call" | custom-call | tf_op jit(solution)/shard_map/pallas_call | solution.py:404
  88.2 0.8 copy.8
Async XLA Ops:
  0.0 0.7 copy-start.6
  0.7 0.7 copy-start.7
  3.0 1.2 %copy-start.3 = (bf16[27,128,128]{2,1,0:T(8,128)(2,1)S(1)}, bf16[27,128,128]{2,1,0:T(8,128)(2,1)}, u32[]{:S(2)}) copy-start(bf16[27,128,128]{2,1,0:T(8,128)(2,1)} %w_ref.1) | copy-start | bytes 2654212
  53.8 0.6 copy-start.5
  54.4 20.2 %copy-start = (bf16[27,128,256]{2,1,0:T(8,128)(2,1)S(1)}, bf16[27,128,256]{2,1,0:T(8,128)(2,1)}, u32[]{:S(2)}) copy-start(bf16[27,128,256]{2,1,0:T(8,128)(2,1)} %param.11) | copy-start | bytes 5308420
  74.7 1.4 %copy-start.1 = (bf16[16,128,384]{2,1,0:T(8,128)(2,1)S(1)}, bf16[16,128,384]{2,1,0:T(8,128)(2,1)}, u32[]{:S(2)}) copy-start(bf16[16,128,384]{2,1,0:T(8,128)(2,1)} %get-tuple-element.18.even_ref) | copy-start | bytes 4718596
  76.1 1.4 %copy-start.2 = (bf16[16,128,384]{2,1,0:T(8,128)(2,1)S(1)}, bf16[16,128,384]{2,1,0:T(8,128)(2,1)}, u32[]{:S(2)}) copy-start(bf16[16,128,384]{2,1,0:T(8,128)(2,1)} %get-tuple-element.19.odd_ref) | copy-start | bytes 4718596
  77.5 0.9 %copy-start.4 = (bf16[128,384]{1,0:T(8,128)(2,1)S(1)}, bf16[128,384]{1,0:T(8,128)(2,1)}, u32[]{:S(2)}) copy-start(bf16[128,384]{1,0:T(8,128)(2,1)} %get-tuple-element.20.last_ref) | copy-start | bytes 294916
where the time goes:
time: 89.4 us; the launch traced here: 89 us
  Pallas kernels  81.3 us (91%)
  local copies, waits for them, and re-layouts  7.72 us (9%)
    pallas_call x1, Pallas kernels, exchange(): pl.pallas_call(exchange_kernel, out_shape=(jax.ShapeDtypeStruct((DEV, CAP...  49.6 us
    pallas_call x1, Pallas kernels, scatter(): pl.pallas_call(scatter_kernel, out_shape=(jax.ShapeDtypeStruct((NX, 128,...  20.2 us
    pallas_call x1, Pallas kernels, lower(): pl.pallas_call(lower_kernel, out_shape=jax.ShapeDtypeStruct((NX // 2, 128...  9.87 us
    unnamed x17, local copies, waits for them, and re-layouts  7.72 us

commit v1 on v0

--- a/solution.py
+++ b/solution.py
@@ -12,13 +12,14 @@
 DEV, CAP, ROWS, C = 128, 64, 4096, 128
 NX, NY, NZ = 16, 32, 16
 CELLS = NX * NY * NZ
-CHAINS = 4
+CHAINS = 8
 VMEM = pl.BlockSpec(memory_space=pltpu.VMEM)
 SMEM = pl.BlockSpec(memory_space=pltpu.SMEM)
 ANY = pl.BlockSpec(memory_space=pl.ANY)
-
-
-def slots_kernel(own_ref, cell_ref, idx_ref, cells_ref, hit_ref, val_ref):
+HBM = pl.BlockSpec(memory_space=pltpu.HBM)
+
+
+def find_slots(own_ref, cell_ref, hit_ref, val_ref, idx_ref, cells_ref):
     block = 256
     hit_ref[...] = (lax.broadcasted_iota(I32, (DEV, ROWS), 0) == own_ref[...]).astype(F32).astype(BF16)
     before = (
@@ -33,33 +34,18 @@
         rank = jnp.sum(ranks * hit32, axis=0, keepdims=True).astype(I32)
         carry = carry + jnp.sum(hit32, axis=1, keepdims=True)
         place = lax.broadcasted_iota(I32, (CAP, block), 0) == rank
-        row = lax.broadcasted_iota(I32, (1, block), 1) + b * block
+        row = lax.broadcasted_iota(I32, (1, block), 1) + b * block + 8
         cell = cell_ref[:, span]
-        for part, value in enumerate((row % 64, row // 64, cell % 64, cell // 64 + 1)):
+        for part, value in enumerate((row % 64, row // 64, cell % 64, cell // 64)):
             chosen = jnp.where(place, value.astype(F32), 0.0)
             val_ref[part * CAP : (part + 1) * CAP, span] = chosen.astype(BF16)
     found = lax.dot_general(
         hit_ref[...], val_ref[...], (((1,), (1,)), ((), ())), preferred_element_type=F32
     ).astype(I32)
-    idx_ref[...] = found[:, CAP : 2 * CAP] * 64 + found[:, :CAP]
-    high = found[:, 3 * CAP :]
-    cell = (high - 1) * 64 + found[:, 2 * CAP : 3 * CAP]
-    cells_ref[:, :CAP] = jnp.where(high > 0, cell, CELLS)
-    cells_ref[:, CAP:] = jnp.full((DEV, CAP), CELLS, I32)
-
-
-def find_slots(own, cell):
-    return pl.pallas_call(
-        slots_kernel,
-        out_shape=(
-            jax.ShapeDtypeStruct((DEV, CAP), I32),
-            jax.ShapeDtypeStruct((DEV, 2 * CAP), I32),
-        ),
-        in_specs=[VMEM, VMEM],
-        out_specs=(VMEM, VMEM),
-        scratch_shapes=[pltpu.VMEM((DEV, ROWS), BF16), pltpu.VMEM((4 * CAP, ROWS), BF16)],
-        compiler_params=pltpu.CompilerParams(vmem_limit_bytes=32 << 20),
-    )(own, cell)
+    idx_ref[:, :CAP] = jnp.clip(found[:, CAP : 2 * CAP] * 64 + found[:, :CAP], 0, ROWS + 7)
+    idx_ref[:, CAP:] = jnp.zeros((DEV, CAP), I32)
+    cells = found[:, 3 * CAP :] * 64 + found[:, 2 * CAP : 3 * CAP]
+    cells_ref[...] = jnp.concatenate([cells, jnp.zeros((DEV, CAP), I32)], axis=1).reshape(DEV, 1, 2 * CAP)
 
 
 def partner(k, p, n):
@@ -69,25 +55,46 @@
 
 
 def exchange_kernel(
-    idx_ref, cells_ref, pts_ref, level_ref, w_ref,
-    got_ref, got_cells_ref, base_ref,
-    rows32, packed, ext, s0, s1, s2, wide, base,
-    row_send, row_recv, cell_send, cell_recv, own_sem, own_cell_sem, in_sem, halo_send, halo_recv, out_sem,
+    own_hbm, cell_hbm, pts_hbm, level_ref, w_hbm,
+    got_ref, got_cells_ref, base,
+    owner_of, cell_of, hit, val, idx_vmem, idx_ref, cells_ref, pts, taps, rows32, packed, ext, s0, s1, s2, wide,
+    row_send, row_recv, cell_send, cell_recv, own_sem, own_cell_sem, in_sem, pts_sem, taps_sem, list_sem, halo_send, halo_recv,
 ):
     p, n = lax.axis_index("pts"), lax.axis_index("nbr")
     n_p, n_n = lax.axis_size("pts"), lax.axis_size("nbr")
     me = p * n_n + n
     barrier = pltpu.get_barrier_semaphore()
+    lists_in = [
+        pltpu.make_async_copy(own_hbm, owner_of, list_sem.at[0]),
+        pltpu.make_async_copy(cell_hbm, cell_of, list_sem.at[1]),
+    ]
+    pts_in = pltpu.make_async_copy(pts_hbm, pts, pts_sem)
+    for copy in lists_in:
+        copy.start()
+    pts_in.start()
 
     def greet(k, carry):
-        tp, tn = partner(k, p, n)
-        pl.semaphore_signal(barrier, inc=1, device_id=(tp, tn), device_id_type=MESH)
-        return carry
-
-    lax.fori_loop(1, DEV, greet, 0)
+        for d in range(n_n):
+            device = ((p + k) % n_p, (n + d) % n_n)
+            pl.semaphore_signal(barrier, inc=1, device_id=device, device_id_type=MESH)
+        return carry
+
+    for d in range(1, n_n):
+        pl.semaphore_signal(barrier, inc=1, device_id=(p, (n + d) % n_n), device_id_type=MESH)
+    lax.fori_loop(1, n_p, greet, 0)
     inner = pltpu.make_async_copy(level_ref, ext.at[pl.ds(1, NX), pl.ds(1, NY)], in_sem)
     inner.start()
-    rows32[...] = pts_ref[...].astype(F32)
+    taps_in = pltpu.make_async_copy(w_hbm, taps, taps_sem)
+    taps_in.start()
+    for copy in lists_in:
+        copy.wait()
+    find_slots(owner_of, cell_of, hit, val, idx_vmem, cells_ref)
+    idx_in = pltpu.make_async_copy(idx_vmem, idx_ref, list_sem.at[2])
+    idx_in.start()
+    rows32[:8, :] = jnp.zeros((8, C), F32)
+    pts_in.wait()
+    rows32[8:, :] = pts[...].astype(F32)
+    idx_in.wait()
 
     def gather(owner):
         for g in range(CAP // 16):
@@ -139,6 +146,7 @@
 
     lax.fori_loop(1, DEV, send, 0)
 
+    taps_in.wait()
     for a in range(3):
         for q in range(2):
             for c in range(3):
@@ -146,7 +154,7 @@
                     for pout in range(2):
                         b = 2 * q + pin - pout
                         at = (a * 2 + q) * 3 + c
-                        tap = w_ref[9 * a + 3 * b + c] if 0 <= b <= 2 else jnp.zeros((C, C), BF16)
+                        tap = taps[9 * a + 3 * b + c] if 0 <= b <= 2 else jnp.zeros((C, C), BF16)
                         wide[at * 256 + pin * C : at * 256 + (pin + 1) * C, pout * C : (pout + 1) * C] = tap
 
     inner.wait()
@@ -192,12 +200,10 @@
         high = s1[i + 1, 1:, :, :C].astype(F32)
         base[i, :, 0] = both[:, :C].reshape(half, NZ, C) + low
         base[i, :, 1] = both[:, C:].reshape(half, NZ, C) + high
-        pltpu.make_async_copy(base.at[i], base_ref.at[i], out_sem).start()
         return carry
 
     lax.fori_loop(0, NX, conv, 0)
 
-    pltpu.make_async_copy(base, base_ref, out_sem).wait()
     own.wait()
     own_cells.wait()
     for there, here, copy, tx, ty in sides:
@@ -213,7 +219,7 @@
     pltpu.make_async_copy(cells_ref.at[most], got_cells_ref.at[most], cell_recv).wait()
 
 
-def exchange(idx, cells, pts, level, w_res):
+def exchange(own, cell, pts, level, w_res):
     dma = pltpu.SemaphoreType.DMA
     padded = (NX + 2, NY // 2 + 1, NZ, 2 * C)
     return pl.pallas_call(
@@ -223,44 +229,49 @@
             jax.ShapeDtypeStruct((DEV, 1, 2 * CAP), I32),
             jax.ShapeDtypeStruct((NX, NY // 2, 2, NZ, C), F32),
         ),
-        in_specs=[SMEM, VMEM, VMEM, ANY, VMEM],
-        out_specs=(ANY, ANY, ANY),
+        in_specs=[HBM, HBM, HBM, HBM, HBM],
+        out_specs=(VMEM, VMEM, VMEM),
         scratch_shapes=[
-            pltpu.VMEM((ROWS, C), F32),
+            pltpu.VMEM((1, ROWS), I32),
+            pltpu.VMEM((1, ROWS), I32),
+            pltpu.VMEM((DEV, ROWS), BF16),
+            pltpu.VMEM((4 * CAP, ROWS), BF16),
+            pltpu.VMEM((DEV, 2 * CAP), I32),
+            pltpu.SMEM((DEV, 2 * CAP), I32),
+            pltpu.VMEM((DEV, 1, 2 * CAP), I32),
+            pltpu.VMEM((ROWS, C), BF16),
+            pltpu.VMEM((27, C, C), BF16),
+            pltpu.VMEM((ROWS + 8, C), F32),
             pltpu.VMEM((DEV, CAP, C), BF16),
             pltpu.VMEM((NX + 2, NY + 2, NZ, C), BF16),
             pltpu.VMEM(padded, BF16),
             pltpu.VMEM(padded, BF16),
             pltpu.VMEM(padded, BF16),
             pltpu.VMEM((18 * 256, 256), BF16),
-            pltpu.VMEM((NX, NY // 2, 2, NZ, C), F32),
-            dma, dma, dma, dma, dma, dma, dma, dma((8,)), dma((8,)), dma,
+            dma, dma, dma, dma, dma, dma, dma, dma, dma, dma((3,)), dma((8,)), dma((8,)),
         ],
         compiler_params=pltpu.CompilerParams(
-            collective_id=0, has_side_effects=True, vmem_limit_bytes=52 << 20
+            collective_id=0, has_side_effects=True, vmem_limit_bytes=36 << 20
         ),
-    )(idx, cells, pts, level, w_res)
-
-
-def scatter_kernel(cells_ref, got_ref, base_ref, even_ref, odd_ref, last_ref, rows32, sem, *sums):
-    first = pltpu.make_async_copy(base_ref, sums[0].at[pl.ds(0, CELLS)], sem)
-    first.start()
+    )(*(pltpu.with_memory_space_constraint(x, pltpu.HBM) for x in (own, cell, pts, level, w_res)))
+
+
+def scatter_kernel(cells_ref, got_ref, base_ref, even_ref, odd_ref, last_ref, rows32, *sums):
 
     def clear(t, carry):
         span = pl.ds(pl.multiple_of(t * 32, 32), 32)
-        for total in sums[1:]:
+        for total in sums:
             total[span, :] = jnp.zeros((32, C), F32)
         rows32[span, :] = got_ref[span, :].astype(F32)
         return carry
 
     lax.fori_loop(0, CELLS // 32, clear, 0)
-    first.wait()
     share = DEV // CHAINS
 
     def add(s, carry):
         for g in range(CAP // 16):
             for r in range(g * 16, g * 16 + 16):
-                at = [cells_ref[k * share + s, r] for k in range(CHAINS)]
+                at = [cells_ref[(k * share + s) * (2 * CAP) + r] for k in range(CHAINS)]
                 new = [
                     sums[k][pl.ds(at[k], 1), :] + rows32[pl.ds((k * share + s) * CAP + r, 1), :]
                     for k in range(CHAINS)
@@ -276,8 +287,8 @@
 
         def total(y, start):
             at = pl.ds((x * NY + y) * NZ + start, NZ // 2, stride=2)
-            value = sums[0][at, :]
-            for more in sums[1:]:
+            value = base_ref[at, :]
+            for more in sums:
                 value = value + more[at, :]
             return value
 
@@ -307,17 +318,16 @@
             jax.ShapeDtypeStruct((NX, 128, 3 * C), BF16),
             jax.ShapeDtypeStruct((128, 3 * C), BF16),
         ),
-        in_specs=[SMEM, VMEM, ANY],
+        in_specs=[SMEM, VMEM, VMEM],
         out_specs=(VMEM, VMEM, VMEM),
-        scratch_shapes=[pltpu.VMEM((CELLS, C), F32), pltpu.SemaphoreType.DMA]
-        + [pltpu.VMEM((CELLS + 8, C), F32)] * CHAINS,
-        compiler_params=pltpu.CompilerParams(vmem_limit_bytes=56 << 20),
+        scratch_shapes=[pltpu.VMEM((CELLS, C), F32)] * (1 + CHAINS),
+        compiler_params=pltpu.CompilerParams(vmem_limit_bytes=40 << 20),
     )(cells, got, base)
 
 
 def lower_kernel(
     even_ref, odd_ref, last_ref, w_ref, out_ref,
-    t0, t1, t2, side, corner, send_sem, recv_sem, in_sem,
+    behind_odd, front_even, front_odd, side, corner, total, send_sem, recv_sem,
 ):
     p, n = lax.axis_index("pts"), lax.axis_index("nbr")
     n_p, n_n = lax.axis_size("pts"), lax.axis_size("nbr")
@@ -330,8 +340,8 @@
     pl.semaphore_wait(barrier, 3)
 
     sent = [
-        (0, even_ref.at[NX - 1], t1.at[0]),
-        (0, odd_ref.at[NX - 1], t2.at[0]),
+        (0, even_ref.at[NX - 1], front_even),
+        (0, odd_ref.at[NX - 1], front_odd),
         (1, last_ref, side),
         (2, last_ref.at[pl.ds(112, 16)], corner),
     ]
@@ -349,14 +359,32 @@
         def _():
             copy.start()
 
-    inner = [
-        pltpu.make_async_copy(even_ref, t1.at[pl.ds(1, NX)], in_sem.at[0]),
-        pltpu.make_async_copy(odd_ref, t2.at[pl.ds(1, NX)], in_sem.at[1]),
-    ]
-    for copy in inner:
-        copy.start()
-    for copy in inner:
-        copy.wait()
+    taps = 3 * C
+
+    def inner(x):
+        return jnp.concatenate([even_ref[x], odd_ref[x]], axis=1)
+
+    def weights(a):
+        return w_ref[(3 * a + 1) * taps : (3 * a + 3) * taps, :]
+
+    for i in range(0, NX // 2, 2):
+        acc = jnp.zeros((256, 2 * C), F32)
+        for a in (1, 2):
+            lhs = jnp.concatenate([inner(2 * i + a - 1), inner(2 * i + a + 1)], axis=0)
+            acc = acc + jnp.dot(lhs, weights(a), preferred_element_type=F32)
+        if i:
+            lhs = jnp.concatenate([inner(2 * i - 1), inner(2 * i + 1)], axis=0)
+            acc = acc + jnp.dot(lhs, weights(0), preferred_element_type=F32)
+            total[i] = acc[:128]
+            total[i + 1] = acc[128:]
+        else:
+            total[0] = acc[:128]
+            total[1] = acc[128:] + jnp.dot(inner(1), weights(0), preferred_element_type=F32)
+
+    for x in range(NX):
+        line = odd_ref[x].astype(F32)
+        behind_odd[x + 1, 16:, :] = line[8:120].astype(BF16)
+
     for there, here, copy, target in copies:
 
         @pl.when(here)
@@ -367,31 +395,28 @@
         def _():
             target[...] = jnp.zeros(target.shape, BF16)
 
-    def behind(x, edge):
-        line = t2[x].astype(F32)
-        t0[x] = jnp.concatenate([edge, line[:120]], axis=0).astype(BF16)
-
-    behind(0, corner[...].astype(F32)[8:])
+    front = front_odd[...].astype(F32)
+    behind_odd[0] = jnp.concatenate([corner[...].astype(F32)[8:], front[:120]], axis=0).astype(BF16)
     for x in range(0, NX, 2):
         edges = side[x * 8 : x * 8 + 16, :].astype(F32)
-        behind(x + 1, edges[:8])
-        behind(x + 2, edges[8:])
-
-    def conv(i, carry):
+        for h in range(2):
+            line = odd_ref[x + h, 0:16, :].astype(F32)[:8]
+            behind_odd[x + h + 1, 0:16, :] = jnp.concatenate([edges[8 * h : 8 * h + 8], line], axis=0).astype(BF16)
+
+    ahead = jnp.concatenate([front_even[...], front_odd[...]], axis=1)
+    total[0] += jnp.dot(ahead, weights(0), preferred_element_type=F32)
+    for i in range(0, NX // 2, 2):
         lhs = jnp.concatenate(
             [
-                jnp.concatenate([t[4 * i + a], t[4 * i + 2 + a]], axis=0)
+                jnp.concatenate([behind_odd[2 * i + a], behind_odd[2 * i + 2 + a]], axis=0)
                 for a in range(3)
-                for t in (t0, t1, t2)
             ],
             axis=1,
         )
-        low = jnp.dot(lhs, w_ref[...], preferred_element_type=F32).astype(BF16)
-        out_ref[2 * i] = low[:128]
-        out_ref[2 * i + 1] = low[128:]
-        return carry
-
-    lax.fori_loop(0, NX // 4, conv, 0)
+        rest = jnp.concatenate([w_ref[3 * a * taps : (3 * a + 1) * taps, :] for a in range(3)], axis=0)
+        low = jnp.dot(lhs, rest, preferred_element_type=F32)
+        out_ref[i] = (total[i] + low[:128]).astype(BF16)
+        out_ref[i + 1] = (total[i + 1] + low[128:]).astype(BF16)
     for there, here, copy, target in copies:
 
         @pl.when(there)
@@ -404,23 +429,30 @@
     return pl.pallas_call(
         lower_kernel,
         out_shape=jax.ShapeDtypeStruct((NX // 2, 128, 2 * C), BF16),
-        in_specs=[ANY, ANY, ANY, VMEM],
+        in_specs=[VMEM, VMEM, VMEM, VMEM],
         out_specs=VMEM,
-        scratch_shapes=[pltpu.VMEM((NX + 1, 128, 3 * C), BF16)] * 3
-        + [pltpu.VMEM((128, 3 * C), BF16), pltpu.VMEM((16, 3 * C), BF16), dma((4,)), dma((4,)), dma((2,))],
+        scratch_shapes=[
+            pltpu.VMEM((NX + 1, 128, 3 * C), BF16),
+            pltpu.VMEM((128, 3 * C), BF16),
+            pltpu.VMEM((128, 3 * C), BF16),
+            pltpu.VMEM((128, 3 * C), BF16),
+            pltpu.VMEM((16, 3 * C), BF16),
+            pltpu.VMEM((NX // 2, 128, 2 * C), F32),
+            dma((4,)),
+            dma((4,)),
+        ],
         compiler_params=pltpu.CompilerParams(
-            collective_id=1, has_side_effects=True, vmem_limit_bytes=48 << 20
+            collective_id=1, has_side_effects=True, vmem_limit_bytes=24 << 20
         ),
     )(even, odd, last, w_down)
 
 
 def body(points, dest_owner, dest_cell, level_input, w_res, w_down):
-    idx, cells = find_slots(dest_owner.reshape(1, ROWS), dest_cell.reshape(1, ROWS))
     got, got_cells, base = exchange(
-        idx, cells.reshape(DEV, 1, 2 * CAP), points.reshape(ROWS, C), level_input, w_res
+        dest_owner.reshape(1, ROWS), dest_cell.reshape(1, ROWS), points.reshape(ROWS, C), level_input, w_res
     )
     even, odd, last = scatter(
-        got_cells.reshape(DEV, 2 * CAP), got.reshape(DEV * CAP, C), base.reshape(CELLS, C)
+        got_cells.reshape(DEV * 2 * CAP), got.reshape(DEV * CAP, C), base.reshape(CELLS, C)
     )
     lowered = lower(even, odd, last, w_down.reshape(27 * C, 2 * C))
     return lowered.reshape(NX // 2, NY // 2, NZ // 2, 2 * C)

time: 89.4 us -> 62.5 us (0.70)
  Pallas kernels: 81.3 us -> 61.2 us
  local copies, waits for them, and re-layouts: 7.72 us -> 0.8 us
    pallas_call x1, Pallas kernels: 49.6 us -> 36.4 us  [exchange(): pl.pallas_call(exchange_kernel, out_shape=(jax.ShapeDtypeStruct((DEV, CAP...]
    unnamed x17 -> x3, local copies, waits for them, and re-layouts: 7.72 us -> 0.8 us
    pallas_call x1, Pallas kernels: 20.2 us -> 13.6 us  [scatter(): pl.pallas_call(scatter_kernel, out_shape=(jax.ShapeDtypeStruct((NX, 128,...]
    pallas_call x1 -> x0, Pallas kernels: 1.54 us -> none  [find_slots(): pl.pallas_call(slots_kernel, out_shape=(jax.ShapeDtypeStruct((DEV, CAP),...]
    pallas_call x1, Pallas kernels: 9.87 us -> 11.2 us  [lower(): pl.pallas_call(lower_kernel, out_shape=jax.ShapeDtypeStruct((NX // 2, 128...]
where the time goes in v1:
time: 62.5 us; the launch traced here: 62 us
  Pallas kernels  61.2 us (98%)
  local copies, waits for them, and re-layouts  0.8 us (1%)
    pallas_call x1, Pallas kernels, exchange(): pl.pallas_call(exchange_kernel, out_shape=(jax.ShapeDtypeStruct((DEV, CAP...  36.4 us
    pallas_call x1, Pallas kernels, scatter(): pl.pallas_call(scatter_kernel, out_shape=(jax.ShapeDtypeStruct((NX, 128,...  13.6 us
    pallas_call x1, Pallas kernels, lower(): pl.pallas_call(lower_kernel, out_shape=jax.ShapeDtypeStruct((NX // 2, 128...  11.2 us

profile of v1, /device:TPU:11, one launch (start us, length us, event | category | flops | bytes accessed | tf_op | source)
XLA Modules:
  0.0 62.0 jit_solution(434608930427657291)
XLA Ops:
  0.0 36.4 %shard_map.64 = (bf16[128,64,128]{2,1,0:T(8,128)(2,1)S(1)}, s32[128,1,128]{2,1,0:T(1,128)S(1)}, f32[16,16,2,16,128]{4,3,2,1,0:T(8,128)S(1)}) custom-call(s32[1,4096]{1,0:T(1,128)} %bitcast.14, s32[1,4096]{1,0:T(1,128)} %bitcast.15, bf16[4096,128]{1,0:T(8,128)(2,1)} %bitcast.13, bf16[16,32,16,128]{3,2,1,0:T(8,128)(2,1)} %level_ref.1, bf16[27,128,128]{2,1,0:T(8,128)(2,1)} %w_hbm.1), custom_call_target="tpu_custom_call" | custom-call | tf_op jit(solution)/shard_map/pallas_call | solution.py:225
  36.4 0.0 copy-start
  36.4 13.6 %shard_map.65 = (bf16[16,128,384]{2,1,0:T(8,128)(2,1)S(1)}, bf16[16,128,384]{2,1,0:T(8,128)(2,1)S(1)}, bf16[128,384]{1,0:T(8,128)(2,1)S(1)}) custom-call(s32[16384]{0:T(1024)S(1)} %bitcast.12, bf16[8192,128]{1,0:T(8,128)(2,1)S(1)} %bitcast.9, f32[8192,128]{1,0:T(8,128)S(1)} %bitcast.8), custom_call_target="tpu_custom_call" | custom-call | tf_op jit(solution)/shard_map/pallas_call | solution.py:314
  50.0 0.0 copy-done
  50.0 11.2 %shard_map.66 = bf16[8,128,256]{2,1,0:T(8,128)(2,1)S(1)} custom-call(bf16[16,128,384]{2,1,0:T(8,128)(2,1)S(1)} %get-tuple-element.14.even_ref, bf16[16,128,384]{2,1,0:T(8,128)(2,1)S(1)} %get-tuple-element.15.odd_ref, bf16[128,384]{1,0:T(8,128)(2,1)S(1)} %get-tuple-element.16.last_ref, bf16[3456,256]{1,0:T(8,128)(2,1)S(1)} %bitcast.11), custom_call_target="tpu_custom_call" | custom-call | tf_op jit(solution)/shard_map/pallas_call | solution.py:429
  61.2 0.8 %copy.8 = bf16[8,16,8,256]{3,2,1,0:T(8,128)(2,1)} copy(bf16[8,16,8,256]{3,2,1,0:T(8,128)(2,1)S(1)} %bitcast.10) | data formatting | bytes 1048576
Async XLA Ops:
  36.4 13.6 %copy-start = (bf16[27,128,256]{2,1,0:T(8,128)(2,1)S(1)}, bf16[27,128,256]{2,1,0:T(8,128)(2,1)}, u32[]{:S(2)}) copy-start(bf16[27,128,256]{2,1,0:T(8,128)(2,1)} %param.11) | copy-start | bytes 5308420

commit v2 on v1

--- a/solution.py
+++ b/solution.py
@@ -45,6 +45,8 @@
     idx_ref[:, :CAP] = jnp.clip(found[:, CAP : 2 * CAP] * 64 + found[:, :CAP], 0, ROWS + 7)
     idx_ref[:, CAP:] = jnp.zeros((DEV, CAP), I32)
     cells = found[:, 3 * CAP :] * 64 + found[:, 2 * CAP : 3 * CAP]
+    full = found[:, CAP : 2 * CAP] + found[:, :CAP] > 0
+    cells = jnp.where(full, cells, lax.broadcasted_iota(I32, (DEV, CAP), 1) * NZ)
     cells_ref[...] = jnp.concatenate([cells, jnp.zeros((DEV, CAP), I32)], axis=1).reshape(DEV, 1, 2 * CAP)
 
 
@@ -256,7 +258,9 @@
     )(*(pltpu.with_memory_space_constraint(x, pltpu.HBM) for x in (own, cell, pts, level, w_res)))
 
 
-def scatter_kernel(cells_ref, got_ref, base_ref, even_ref, odd_ref, last_ref, rows32, *sums):
+def scatter_kernel(cells_in, got_ref, base_ref, even_ref, odd_ref, last_ref, cells_ref, sem, rows32, *sums):
+    listed = pltpu.make_async_copy(cells_in, cells_ref, sem)
+    listed.start()
 
     def clear(t, carry):
         span = pl.ds(pl.multiple_of(t * 32, 32), 32)
@@ -267,6 +271,7 @@
 
     lax.fori_loop(0, CELLS // 32, clear, 0)
     share = DEV // CHAINS
+    listed.wait()
 
     def add(s, carry):
         for g in range(CAP // 16):
@@ -306,7 +311,7 @@
 
     lax.fori_loop(0, NX, deal, 0)
     for x in range(0, NX, 2):
-        parts = [odd_ref[x + h, 112:128, :].astype(F32)[8:] for h in range(2)]
+        parts = [odd_ref[x + h, 112:128, C:].astype(F32)[8:] for h in range(2)]
         last_ref[x * 8 : x * 8 + 16, :] = jnp.concatenate(parts, axis=0).astype(BF16)
 
 
@@ -316,18 +321,19 @@
         out_shape=(
             jax.ShapeDtypeStruct((NX, 128, 3 * C), BF16),
             jax.ShapeDtypeStruct((NX, 128, 3 * C), BF16),
-            jax.ShapeDtypeStruct((128, 3 * C), BF16),
+            jax.ShapeDtypeStruct((128, 2 * C), BF16),
         ),
-        in_specs=[SMEM, VMEM, VMEM],
+        in_specs=[ANY, VMEM, VMEM],
         out_specs=(VMEM, VMEM, VMEM),
-        scratch_shapes=[pltpu.VMEM((CELLS, C), F32)] * (1 + CHAINS),
+        scratch_shapes=[pltpu.SMEM((DEV * 2 * CAP,), I32), pltpu.SemaphoreType.DMA]
+        + [pltpu.VMEM((CELLS, C), F32)] * (1 + CHAINS),
         compiler_params=pltpu.CompilerParams(vmem_limit_bytes=40 << 20),
     )(cells, got, base)
 
 
 def lower_kernel(
     even_ref, odd_ref, last_ref, w_ref, out_ref,
-    behind_odd, front_even, front_odd, side, corner, total, send_sem, recv_sem,
+    behind, front_even, front_odd, side, corner, first, heads, send_sem, recv_sem,
 ):
     p, n = lax.axis_index("pts"), lax.axis_index("nbr")
     n_p, n_n = lax.axis_size("pts"), lax.axis_size("nbr")
@@ -340,8 +346,8 @@
     pl.semaphore_wait(barrier, 3)
 
     sent = [
-        (0, even_ref.at[NX - 1], front_even),
-        (0, odd_ref.at[NX - 1], front_odd),
+        (0, even_ref.at[NX - 1, :, pl.ds(C, 2 * C)], front_even),
+        (0, odd_ref.at[NX - 1, :, pl.ds(C, 2 * C)], front_odd),
         (1, last_ref, side),
         (2, last_ref.at[pl.ds(112, 16)], corner),
     ]
@@ -360,30 +366,29 @@
             copy.start()
 
     taps = 3 * C
-
-    def inner(x):
-        return jnp.concatenate([even_ref[x], odd_ref[x]], axis=1)
-
-    def weights(a):
-        return w_ref[(3 * a + 1) * taps : (3 * a + 3) * taps, :]
-
-    for i in range(0, NX // 2, 2):
-        acc = jnp.zeros((256, 2 * C), F32)
-        for a in (1, 2):
-            lhs = jnp.concatenate([inner(2 * i + a - 1), inner(2 * i + a + 1)], axis=0)
-            acc = acc + jnp.dot(lhs, weights(a), preferred_element_type=F32)
-        if i:
-            lhs = jnp.concatenate([inner(2 * i - 1), inner(2 * i + 1)], axis=0)
-            acc = acc + jnp.dot(lhs, weights(0), preferred_element_type=F32)
-            total[i] = acc[:128]
-            total[i + 1] = acc[128:]
-        else:
-            total[0] = acc[:128]
-            total[1] = acc[128:] + jnp.dot(inner(1), weights(0), preferred_element_type=F32)
-
     for x in range(NX):
         line = odd_ref[x].astype(F32)
-        behind_odd[x + 1, 16:, :] = line[8:120].astype(BF16)
+        behind[x] = jnp.concatenate([jnp.zeros((8, taps), F32), line[:120]], axis=0).astype(BF16)
+
+    def held(x):
+        return jnp.concatenate([behind[x], even_ref[x], odd_ref[x]], axis=1)
+
+    for i in range(0, NX // 2, 2):
+        lhs = [
+            jnp.concatenate([held(2 * i + a - 1), held(2 * i + a + 1)], axis=0)
+            for a in range(0 if i else 1, 3)
+        ]
+        weights = w_ref[...] if i else w_ref[3 * taps :, :]
+        acc = jnp.dot(jnp.concatenate(lhs, axis=1), weights, preferred_element_type=F32)
+        low, high = acc[:128], acc[128:]
+        if i == 0:
+            first[...] = low
+            high = high + jnp.dot(held(1), w_ref[: 3 * taps, :], preferred_element_type=F32)
+        else:
+            heads[i] = low[:16]
+            out_ref[i] = low.astype(BF16)
+        heads[i + 1] = high[:16]
+        out_ref[i + 1] = high.astype(BF16)
 
     for there, here, copy, target in copies:
 
@@ -395,28 +400,37 @@
         def _():
             target[...] = jnp.zeros(target.shape, BF16)
 
-    front = front_odd[...].astype(F32)
-    behind_odd[0] = jnp.concatenate([corner[...].astype(F32)[8:], front[:120]], axis=0).astype(BF16)
-    for x in range(0, NX, 2):
-        edges = side[x * 8 : x * 8 + 16, :].astype(F32)
-        for h in range(2):
-            line = odd_ref[x + h, 0:16, :].astype(F32)[:8]
-            behind_odd[x + h + 1, 0:16, :] = jnp.concatenate([edges[8 * h : 8 * h + 8], line], axis=0).astype(BF16)
-
-    ahead = jnp.concatenate([front_even[...], front_odd[...]], axis=1)
-    total[0] += jnp.dot(ahead, weights(0), preferred_element_type=F32)
-    for i in range(0, NX // 2, 2):
-        lhs = jnp.concatenate(
-            [
-                jnp.concatenate([behind_odd[2 * i + a], behind_odd[2 * i + 2 + a]], axis=0)
-                for a in range(3)
-            ],
-            axis=1,
-        )
-        rest = jnp.concatenate([w_ref[3 * a * taps : (3 * a + 1) * taps, :] for a in range(3)], axis=0)
-        low = jnp.dot(lhs, rest, preferred_element_type=F32)
-        out_ref[i] = (total[i] + low[:128]).astype(BF16)
-        out_ref[i + 1] = (total[i + 1] + low[128:]).astype(BF16)
+    def widened(lines):
+        lines = lines.astype(F32).reshape(-1, 8, 2 * C)
+        odd = lines[:, :, C:]
+        below = jnp.concatenate([jnp.zeros((odd.shape[0], 1, C), F32), odd[:, :7]], axis=1)
+        return jnp.concatenate([below, lines], axis=2)
+
+    edge = widened(side[...]).reshape(NX // 2, 2, 8, taps)
+    before = widened(corner[...])[1:]
+    lhs = jnp.concatenate(
+        [jnp.concatenate([before, edge[: NX // 2 - 1, 1]], axis=0), edge[:, 0], edge[:, 1]], axis=2
+    )
+    beside_w = jnp.concatenate([w_ref[3 * a * taps : (3 * a + 1) * taps, :] for a in range(3)], axis=0)
+    beside = jnp.dot(
+        lhs.reshape(NX // 2 * 8, 3 * taps).astype(BF16), beside_w, preferred_element_type=F32
+    )
+    odd = widened(front_odd[...]).reshape(128, taps)
+    lhs = jnp.concatenate(
+        [
+            jnp.concatenate([jnp.zeros((8, taps), F32), odd[:120]], axis=0),
+            widened(front_even[...]).reshape(128, taps),
+            odd,
+        ],
+        axis=1,
+    )
+    ahead = first[...] + jnp.dot(lhs.astype(BF16), w_ref[: 3 * taps, :], preferred_element_type=F32)
+    out_ref[0] = ahead.astype(BF16)
+    heads[0] = ahead[:16]
+    for i in range(NX // 2):
+        head = heads[i]
+        head = jnp.concatenate([head[:8] + beside[8 * i : 8 * i + 8], head[8:]], axis=0)
+        out_ref[i, 0:16, :] = head.astype(BF16)
     for there, here, copy, target in copies:
 
         @pl.when(there)
@@ -432,12 +446,13 @@
         in_specs=[VMEM, VMEM, VMEM, VMEM],
         out_specs=VMEM,
         scratch_shapes=[
-            pltpu.VMEM((NX + 1, 128, 3 * C), BF16),
-            pltpu.VMEM((128, 3 * C), BF16),
-            pltpu.VMEM((128, 3 * C), BF16),
-            pltpu.VMEM((128, 3 * C), BF16),
-            pltpu.VMEM((16, 3 * C), BF16),
-            pltpu.VMEM((NX // 2, 128, 2 * C), F32),
+            pltpu.VMEM((NX, 128, 3 * C), BF16),
+            pltpu.VMEM((128, 2 * C), BF16),
+            pltpu.VMEM((128, 2 * C), BF16),
+            pltpu.VMEM((128, 2 * C), BF16),
+            pltpu.VMEM((16, 2 * C), BF16),
+            pltpu.VMEM((128, 2 * C), F32),
+            pltpu.VMEM((NX // 2, 16, 2 * C), F32),
             dma((4,)),
             dma((4,)),
         ],

time: 62.5 us -> 57.4 us (0.918)
  Pallas kernels: 61.2 us -> 55.9 us
    pallas_call x1, Pallas kernels: 11.2 us -> 7.72 us  [lower(): pl.pallas_call(lower_kernel, out_shape=jax.ShapeDtypeStruct((NX // 2, 128...]
    pallas_call x1, Pallas kernels: 13.6 us -> 11.8 us  [scatter(): pl.pallas_call(scatter_kernel, out_shape=(jax.ShapeDtypeStruct((NX, 128,...]
where the time goes in v2:
time: 57.4 us; the launch traced here: 56.7 us
  Pallas kernels  55.9 us (97%)
  local copies, waits for them, and re-layouts  0.8 us (1%)
    pallas_call x1, Pallas kernels, exchange(): pl.pallas_call(exchange_kernel, out_shape=(jax.ShapeDtypeStruct((DEV, CAP...  36.4 us
    pallas_call x1, Pallas kernels, scatter(): pl.pallas_call(scatter_kernel, out_shape=(jax.ShapeDtypeStruct((NX, 128,...  11.8 us
    pallas_call x1, Pallas kernels, lower(): pl.pallas_call(lower_kernel, out_shape=jax.ShapeDtypeStruct((NX // 2, 128...  7.72 us

profile of v2, /device:TPU:11, one launch (start us, length us, event | category | flops | bytes accessed | tf_op | source)
XLA Modules:
  0.0 56.7 jit_solution(14204504340108982505)
XLA Ops:
  0.0 36.4 %shard_map.64 = (bf16[128,64,128]{2,1,0:T(8,128)(2,1)S(1)}, s32[128,1,128]{2,1,0:T(1,128)S(1)}, f32[16,16,2,16,128]{4,3,2,1,0:T(8,128)S(1)}) custom-call(s32[1,4096]{1,0:T(1,128)} %bitcast.14, s32[1,4096]{1,0:T(1,128)} %bitcast.15, bf16[4096,128]{1,0:T(8,128)(2,1)} %bitcast.13, bf16[16,32,16,128]{3,2,1,0:T(8,128)(2,1)} %level_ref.1, bf16[27,128,128]{2,1,0:T(8,128)(2,1)} %w_hbm.1), custom_call_target="tpu_custom_call" | custom-call | tf_op jit(solution)/shard_map/pallas_call | solution.py:227
  36.4 0.0 copy-start
  36.4 11.8 %shard_map.65 = (bf16[16,128,384]{2,1,0:T(8,128)(2,1)S(1)}, bf16[16,128,384]{2,1,0:T(8,128)(2,1)S(1)}, bf16[128,256]{1,0:T(8,128)(2,1)S(1)}) custom-call(s32[16384]{0:T(1024)S(1)} %bitcast.12, bf16[8192,128]{1,0:T(8,128)(2,1)S(1)} %bitcast.9, f32[8192,128]{1,0:T(8,128)S(1)} %bitcast.8), custom_call_target="tpu_custom_call" | custom-call | tf_op jit(solution)/shard_map/pallas_call | solution.py:319
  48.2 0.0 copy-done
  48.2 7.7 %shard_map.66 = bf16[8,128,256]{2,1,0:T(8,128)(2,1)S(1)} custom-call(bf16[16,128,384]{2,1,0:T(8,128)(2,1)S(1)} %get-tuple-element.14.even_ref, bf16[16,128,384]{2,1,0:T(8,128)(2,1)S(1)} %get-tuple-element.15.odd_ref, bf16[128,256]{1,0:T(8,128)(2,1)S(1)} %get-tuple-element.16.last_ref, bf16[3456,256]{1,0:T(8,128)(2,1)S(1)} %bitcast.11), custom_call_target="tpu_custom_call" | custom-call | tf_op jit(solution)/shard_map/pallas_call | solution.py:443
  55.9 0.8 %copy.8 = bf16[8,16,8,256]{3,2,1,0:T(8,128)(2,1)} copy(bf16[8,16,8,256]{3,2,1,0:T(8,128)(2,1)S(1)} %bitcast.10) | data formatting | bytes 1048576
Async XLA Ops:
  36.4 11.8 %copy-start = (bf16[27,128,256]{2,1,0:T(8,128)(2,1)S(1)}, bf16[27,128,256]{2,1,0:T(8,128)(2,1)}, u32[]{:S(2)}) copy-start(bf16[27,128,256]{2,1,0:T(8,128)(2,1)} %param.11) | copy-start | bytes 5308420

commit v3 on v2

--- a/solution.py
+++ b/solution.py
@@ -13,6 +13,7 @@
 NX, NY, NZ = 16, 32, 16
 CELLS = NX * NY * NZ
 CHAINS = 8
+LAYERS = 4
 VMEM = pl.BlockSpec(memory_space=pltpu.VMEM)
 SMEM = pl.BlockSpec(memory_space=pltpu.SMEM)
 ANY = pl.BlockSpec(memory_space=pl.ANY)
@@ -187,10 +188,11 @@
 
     half = NY // 2
 
-    def conv(i, carry):
+    def conv(t, carry):
+        i = t * LAYERS
         lhs = jnp.concatenate(
             [
-                s[i + a, q : q + half].reshape(half * NZ, 2 * C)
+                s[pl.ds(i + a, LAYERS), q : q + half].reshape(LAYERS * half * NZ, 2 * C)
                 for a in range(3)
                 for q in range(2)
                 for s in (s0, s1, s2)
@@ -198,13 +200,13 @@
             axis=1,
         )
         both = jnp.maximum(jnp.dot(lhs, wide[...], preferred_element_type=F32), 0.0)
-        low = s1[i + 1, :half, :, C:].astype(F32)
-        high = s1[i + 1, 1:, :, :C].astype(F32)
-        base[i, :, 0] = both[:, :C].reshape(half, NZ, C) + low
-        base[i, :, 1] = both[:, C:].reshape(half, NZ, C) + high
-        return carry
-
-    lax.fori_loop(0, NX, conv, 0)
+        low = s1[pl.ds(i + 1, LAYERS), :half, :, C:].astype(F32)
+        high = s1[pl.ds(i + 1, LAYERS), 1:, :, :C].astype(F32)
+        base[pl.ds(i, LAYERS), :, 0] = both[:, :C].reshape(LAYERS, half, NZ, C) + low
+        base[pl.ds(i, LAYERS), :, 1] = both[:, C:].reshape(LAYERS, half, NZ, C) + high
+        return carry
+
+    lax.fori_loop(0, NX // LAYERS, conv, 0)
 
     own.wait()
     own_cells.wait()

time: 57.4 us -> 57.2 us (level)
  no operation moved by 1% of the time
where the time goes in v3:
time: 57.2 us; the launch traced here: 56.6 us
  Pallas kernels  55.8 us (98%)
  local copies, waits for them, and re-layouts  0.8 us (1%)
    pallas_call x1, Pallas kernels, exchange(): pl.pallas_call(exchange_kernel, out_shape=(jax.ShapeDtypeStruct((DEV, CAP...  36 us
    pallas_call x1, Pallas kernels, scatter(): pl.pallas_call(scatter_kernel, out_shape=(jax.ShapeDtypeStruct((NX, 128,...  11.8 us
    pallas_call x1, Pallas kernels, lower(): pl.pallas_call(lower_kernel, out_shape=jax.ShapeDtypeStruct((NX // 2, 128...  8.02 us

profile of v3, /device:TPU:11, one launch (start us, length us, event | category | flops | bytes accessed | tf_op | source)
XLA Modules:
  0.0 56.6 jit_solution(16539240698580658138)
XLA Ops:
  0.0 36.0 %shard_map.64 = (bf16[128,64,128]{2,1,0:T(8,128)(2,1)S(1)}, s32[128,1,128]{2,1,0:T(1,128)S(1)}, f32[16,16,2,16,128]{4,3,2,1,0:T(8,128)S(1)}) custom-call(s32[1,4096]{1,0:T(1,128)} %bitcast.14, s32[1,4096]{1,0:T(1,128)} %bitcast.15, bf16[4096,128]{1,0:T(8,128)(2,1)} %bitcast.13, bf16[16,32,16,128]{3,2,1,0:T(8,128)(2,1)} %level_ref.1, bf16[27,128,128]{2,1,0:T(8,128)(2,1)} %w_hbm.1), custom_call_target="tpu_custom_call" | custom-call | tf_op jit(solution)/shard_map/pallas_call | solution.py:229
  36.0 0.0 copy-start
  36.0 11.8 %shard_map.65 = (bf16[16,128,384]{2,1,0:T(8,128)(2,1)S(1)}, bf16[16,128,384]{2,1,0:T(8,128)(2,1)S(1)}, bf16[128,256]{1,0:T(8,128)(2,1)S(1)}) custom-call(s32[16384]{0:T(1024)S(1)} %bitcast.12, bf16[8192,128]{1,0:T(8,128)(2,1)S(1)} %bitcast.9, f32[8192,128]{1,0:T(8,128)S(1)} %bitcast.8), custom_call_target="tpu_custom_call" | custom-call | tf_op jit(solution)/shard_map/pallas_call | solution.py:321
  47.8 0.0 copy-done
  47.8 8.0 %shard_map.66 = bf16[8,128,256]{2,1,0:T(8,128)(2,1)S(1)} custom-call(bf16[16,128,384]{2,1,0:T(8,128)(2,1)S(1)} %get-tuple-element.14.even_ref, bf16[16,128,384]{2,1,0:T(8,128)(2,1)S(1)} %get-tuple-element.15.odd_ref, bf16[128,256]{1,0:T(8,128)(2,1)S(1)} %get-tuple-element.16.last_ref, bf16[3456,256]{1,0:T(8,128)(2,1)S(1)} %bitcast.11), custom_call_target="tpu_custom_call" | custom-call | tf_op jit(solution)/shard_map/pallas_call | solution.py:445
  55.8 0.8 %copy.8 = bf16[8,16,8,256]{3,2,1,0:T(8,128)(2,1)} copy(bf16[8,16,8,256]{3,2,1,0:T(8,128)(2,1)S(1)} %bitcast.10) | data formatting | bytes 1048576
Async XLA Ops:
  36.0 11.8 %copy-start = (bf16[27,128,256]{2,1,0:T(8,128)(2,1)S(1)}, bf16[27,128,256]{2,1,0:T(8,128)(2,1)}, u32[]{:S(2)}) copy-start(bf16[27,128,256]{2,1,0:T(8,128)(2,1)} %param.11) | copy-start | bytes 5308420
